TPU v7x, 512 devices: a whole 4x8x8 slice. The times are simulated.
512 devices in a mesh: replica: 16 (over x, y_lo), fsdp: 32 (over z, y_hi, core).
Axes of the slice: x: 4, y: 8 (y_hi: 2, y_lo: 4; y = y_hi * 4 + y_lo), z: 8, core: 2. Of those that a mesh axis runs over, the one named last changes fastest.
Arguments:
- tokens: bfloat16 [16, 4096, 256], P('replica', 'fsdp'), may hold values from -6 to 6
- gate_weight: bfloat16 [256, 28672], P(None, 'fsdp'), may hold values from -0.375 to 0.375
- down_weight: bfloat16 [28672, 256], P('fsdp'), may hold values from -0.03125 to 0.03125
- local_up: bfloat16 [16, 256, 28672], P('replica', None, 'fsdp'), may hold values from -6 to 6
- deltas: bfloat16 [16, 256, 28672], P('replica', None, 'fsdp'), may hold values from -6 to 6
- outer_up: float32 [256, 28672], P('replica', 'fsdp'), may hold values from -6 to 6
- momentum: float32 [256, 28672], P('replica', 'fsdp'), may hold values from -3 to 3
Outputs:
- inner_out: bfloat16 [16, 4096, 256], P('replica', 'fsdp')
- merged_up: bfloat16 [16, 256, 28672], P('replica', None, 'fsdp')
- new_outer: float32 [256, 28672], P('replica', 'fsdp')
- new_momentum: float32 [256, 28672], P('replica', 'fsdp')
All inputs are finite; a program needn't handle non-finite values.
Results may differ from a plain program's by a relative error of at most 0.02.
Values may be sent and summed in bfloat16 or wider, within the bound.
A program may use at most 64 MiB of HBM per device.

v0:
```python
import jax
import jax.numpy as jnp
from jax import lax
from jax.sharding import PartitionSpec as P

ROWS = 256


outer_rate = 0.7
momentum_coef = 0.9
mix_weight = 0.5


def inner_pass(tokens, gate_weight, down_weight, up_slab):
    rows = lax.all_gather(tokens, "fsdp", axis=1, tiled=True)[0]
    gate = jnp.dot(rows, gate_weight, preferred_element_type=jnp.float32)
    upper = jnp.dot(rows, up_slab, preferred_element_type=jnp.float32) * ROWS ** (-0.5)
    hidden = (jax.nn.silu(gate) * upper).astype(jnp.bfloat16)
    partial_terms = jnp.dot(hidden, down_weight, preferred_element_type=jnp.float32)[None]
    return lax.psum_scatter(
        partial_terms.astype(jnp.bfloat16), "fsdp", scatter_dimension=1, tiled=True
    )


def outer_sync(deltas, outer_up, momentum):
    summand = deltas[0].astype(jnp.float32)
    full_sum = lax.psum(summand.astype(jnp.bfloat16), "replica").astype(jnp.float32)
    share_rows = outer_up.shape[0]
    offset = lax.axis_index("replica") * share_rows
    total = lax.dynamic_slice_in_dim(full_sum, offset, share_rows, 0)
    grad = total / lax.axis_size("replica")
    new_momentum = momentum_coef * momentum + grad
    new_outer = outer_up - outer_rate * (grad + momentum_coef * new_momentum)
    return (new_outer, new_momentum)


def body(tokens, gate_weight, down_weight, local_up, deltas, outer_up, momentum):
    up_slab = local_up[0]
    inner_out = inner_pass(tokens, gate_weight, down_weight, up_slab)
    new_outer, new_momentum = outer_sync(deltas, outer_up, momentum)
    outer_half = lax.all_gather(new_outer.astype(jnp.bfloat16), "replica", axis=0, tiled=True)
    merged = mix_weight * up_slab.astype(jnp.float32) + (1.0 - mix_weight) * outer_half.astype(
        jnp.float32
    )
    merged_up = merged.astype(jnp.bfloat16)[None]
    return (inner_out, merged_up, new_outer, new_momentum)


def solution(mesh):
    placed = (
        P("replica", "fsdp", None),
        P(None, "fsdp"),
        P("fsdp", None),
        P("replica", None, "fsdp"),
        P("replica", None, "fsdp"),
        P("replica", "fsdp"),
        P("replica", "fsdp"),
    )
    return jax.shard_map(
        body,
        mesh=mesh,
        in_specs=placed,
        out_specs=(
            P("replica", "fsdp", None),
            P("replica", None, "fsdp"),
            P("replica", "fsdp"),
            P("replica", "fsdp"),
        ),
        check_vma=False,
    )
```

profile of v0, /device:TPU:2, one launch (start us, length us, event | category | flops | bytes accessed | tf_op | source)
XLA Modules:
  0.0 268.6 jit_solution(439944284384188583)
XLA Ops:
  8.0 0.0 copy-start
  8.0 0.0 copy-start.2
  8.0 0.0 all-gather.2.cloned.1.call-start
  8.1 0.7 all-gather.2.cloned.1.call-update
  8.8 0.0 all-reduce.2.cloned.1.call-start
  8.8 0.5 all-reduce.2.cloned.1.call-update
  9.3 0.0 reduce-scatter.2.cloned.1.call-start
  9.4 97.8 %all-gather.2.cloned.1.call-done = bf16[1,4096,256]{2,1,0:T(8,128)(2,1)} async-done(((bf16[1,128,256]{2,1,0:T(8,128)(2,1)}), bf16[1,4096,256]{2,1,0:T(8,128)(2,1)}) %all-gather.2.cloned.1.call-update) | async-done | bytes 2097168 | tf_op jit(solution)/shard_map/all_gather | solution.py:15
  107.2 0.0 copy-done
  107.2 0.0 copy-start.1
  107.2 9.3 %fusion.3 = f32[4096,896]{1,0:T(8,128)} fusion(bf16[256,896]{1,0:T(8,128)(2,1)S(1)} %copy-done, bf16[1,4096,256]{2,1,0:T(8,128)(2,1)} %all-gather.2.cloned.1.call-done), kind=kOutput, calls=%fused_computation.4 | convolution fusion | flops 1879048192 | bytes 17235968 | tf_op jit(solution)/shard_map/dot_general | solution.py:16
  116.5 0.0 copy-done.2
  116.5 0.0 copy-done.1
  116.5 0.0 copy-start.3
  116.5 0.0 copy-start.4
  116.5 9.1 %fusion = bf16[1,4096,256]{2,1,0:T(8,128)(2,1)} fusion(bf16[896,256]{1,0:T(8,128)(2,1)} %param.9, f32[4096,896]{1,0:T(8,128)} %fusion.3, bf16[1,4096,256]{2,1,0:T(8,128)(2,1)S(1)} %copy-done.1, bf16[1,256,896]{2,1,0:T(8,128)(2,1)S(1)} %copy-done.2), kind=kOutput, calls=%fused_computation.2 | convolution fusion | flops 3784835072 | bytes 19791872 | tf_op jit(solution)/shard_map/dot_general | solution.py:19
  125.6 0.0 reduce-scatter.2.cloned.1.call-update
  125.6 68.1 %all-reduce.2.cloned.1.call-done = bf16[256,896]{1,0:T(8,128)(2,1)} async-done(((bf16[256,896]{1,0:T(8,128)(2,1)}), bf16[256,896]{1,0:T(8,128)(2,1)}) %all-reduce.2.cloned.1.call-update) | async-done | bytes 458768 | tf_op jit(solution)/shard_map/psum | solution.py:27
  193.7 0.0 copy-done.3
  193.7 0.0 copy-done.4
  193.7 1.4 fusion.10
  195.1 39.8 %all_gather.7 = bf16[256,896]{1,0:T(8,128)(2,1)S(1)} all-gather(bf16[16,896]{1,0:T(8,128)(2,1)S(1)} %get-tuple-element.4), channel_id=1, replica_groups=mesh['replica'=16,'fsdp'=32] {'replica'}, dimensions={0}, use_global_device_ids=true | all-gather | bytes 487424 | tf_op jit(solution)/shard_map/all_gather | solution.py:41
  235.0 0.9 fusion.5
  235.9 25.3 %reduce-scatter.2.cloned.1.call-done = bf16[1,128,256]{2,1,0:T(8,128)(2,1)} async-done(((bf16[1,4096,256]{2,1,0:T(8,128)(2,1)}), bf16[1,128,256]{2,1,0:T(8,128)(2,1)}) %reduce-scatter.2.cloned.1.call-update) | async-done | bytes 65552 | tf_op jit(solution)/shard_map/reduce_scatter | solution.py:20
Async XLA Ops:
  8.0 99.2 %copy-start = (bf16[256,896]{1,0:T(8,128)(2,1)S(1)}, bf16[256,896]{1,0:T(8,128)(2,1)}, u32[]{:S(2)}) copy-start(bf16[256,896]{1,0:T(8,128)(2,1)} %param.8) | copy-start | bytes 1376260
  8.0 108.5 %copy-start.2 = (bf16[1,256,896]{2,1,0:T(8,128)(2,1)S(1)}, bf16[1,256,896]{2,1,0:T(8,128)(2,1)}, u32[]{:S(2)}) copy-start(bf16[1,256,896]{2,1,0:T(8,128)(2,1)} %param.10) | copy-start | bytes 1376260
  8.0 99.2 %all-gather.2.cloned.1.call-start = ((), (), s32[]{:S(2)}) async-start(), calls=%async_computation.1 | async-start | bytes 2162688 | tf_op jit(solution)/shard_map/all_gather | solution.py:15
  8.8 185.0 %all-reduce.2.cloned.1.call-start = ((), (), s32[]{:S(2)}) async-start(), calls=%async_computation.3 | async-start | bytes 917504 | tf_op jit(solution)/shard_map/psum | solution.py:27
  9.3 251.8 %reduce-scatter.2.cloned.1.call-start = ((), (), s32[]{:S(2)}) async-start(), calls=%async_computation.2 | async-start | bytes 2162688 | tf_op jit(solution)/shard_map/reduce_scatter | solution.py:20
  107.2 9.3 %copy-start.1 = (bf16[1,4096,256]{2,1,0:T(8,128)(2,1)S(1)}, bf16[1,4096,256]{2,1,0:T(8,128)(2,1)}, u32[]{:S(2)}) copy-start(bf16[1,4096,256]{2,1,0:T(8,128)(2,1)} %all-gather.2.cloned.1.call-done) | copy-start | bytes 6291460
  116.5 77.2 %copy-start.3 = (f32[16,896]{1,0:T(8,128)S(1)}, f32[16,896]{1,0:T(8,128)}, u32[]{:S(2)}) copy-start(f32[16,896]{1,0:T(8,128)} %param.12) | copy-start | bytes 172036
  116.5 77.2 %copy-start.4 = (f32[16,896]{1,0:T(8,128)S(1)}, f32[16,896]{1,0:T(8,128)}, u32[]{:S(2)}) copy-start(f32[16,896]{1,0:T(8,128)} %param.13) | copy-start | bytes 172036
Sparse Core Ops, SparseCore 0:
  12.2 94.9 all-gather.1
  125.7 135.3 reduce-scatter.1
Sparse Core Ops, SparseCore 1:
  12.4 181.2 all-reduce.1
where the time goes:
time: 269 us
  waiting for transfers between devices  192 us (71%)
  blocking collectives  39.8 us (15%)
  matrix products  18.4 us (7%)
  between operations  15.5 us (6%)
    all_gather x1, waiting for transfers between devices, inner_pass(): rows = lax.all_gather(tokens, 'fsdp', axis=1, tiled=True)[0]  97.8 us
    psum x1, waiting for transfers between devices, outer_sync(): lax.psum(summand.astype(jnp.bfloat16), 'replica').astype(jnp.float32)  68.1 us
    all_gather x1, blocking collectives, body(): lax.all_gather(new_outer.astype(jnp.bfloat16), 'replica', axis=0, tiled=T...  39.8 us
    reduce_scatter x1, waiting for transfers between devices, inner_pass(): lax.psum_scatter(partial_terms.astype(jnp.bfloat16), 'fsdp', scatter_dime...  25.3 us
    dot_general x1, matrix products, inner_pass(): gate = jnp.dot(rows, gate_weight, preferred_element_type=jnp.float32)  9.29 us
    dot_general x1, matrix products, inner_pass(): jnp.dot(hidden, down_weight, preferred_element_type=jnp.float32)[None]  9.07 us
  transfers between devices with their start and end apart: 3, of which 3 were waited for; matrix products, arithmetic and copies ran while one was open for 8% of the time, Pallas kernels for 0%

commit v1 on v0

v1 whole, which is shorter than its diff:
```python
import jax
import jax.numpy as jnp
from jax import lax
from jax.experimental import pallas as pl
from jax.experimental.pallas import tpu as pltpu
from jax.sharding import PartitionSpec as P

MESH = pl.DeviceIdType.MESH
BF16, F32 = jnp.bfloat16, jnp.float32

NX, NYLO, NZ = 4, 4, 8
N_REPLICA = NX * NYLO
ROWS = 256

outer_rate = 0.7
momentum_coef = 0.9
mix_weight = 0.5

OWN, PAR = 0, 1
BASE = ((0, 1, 4, 8, 12), (3, 6, 10, 13, 15))
N_SLOT = 16

GATHER_AT = {
    1: ((OWN, 1),),
    2: ((PAR, 0),),
    3: ((OWN, 2),),
    5: ((PAR, 1),),
    7: ((OWN, 3),),
    9: ((PAR, 2),),
    11: ((OWN, 4),),
    12: ((PAR, 3),),
    14: ((PAR, 4),),
}
REDUCE_AT = {
    11: ((OWN, 1, 3),),
    14: ((OWN, 0, 4),),
    15: ((OWN, 1, 2),),
}
OUTER_AT = {6: 2, 10: 3, 13: 4}


def kernel(
    tokens, gate_w, down_w, local_up, deltas, outer_up, momentum,
    inner_out, merged_up, new_outer, new_momentum,
    tok, gate_v, up_v, down_v, delta_v, outer_v, mom_v,
    part, sib_part, rs_in, rs_out, y_in, own_sum,
    x_in, y_mid, y_sum_in, half_all, merged_v, out_v, no_v, nm_v,
    load_sem, store_sem, ag_send, ag_recv, ag_sib_send, ag_sib_recv,
    ps_send, ps_recv, rs_send, rs_recv, yx_send, yx_recv, o_send, o_recv,
):
    r, f = lax.axis_index("replica"), lax.axis_index("fsdp")
    x, ylo = r // NYLO, r % NYLO
    z, yh, c = f // 4, (f // 2) % 2, f % 2
    a = 1 - 2 * c
    blk = tokens.shape[1]

    def dev(x=x, ylo=ylo, z=z, yh=yh, c=c):
        return (x * NYLO + ylo, z * 4 + yh * 2 + c)

    sibling = dev(c=1 - c)
    partner = dev(yh=1 - yh)
    ahead = (dev(z=(z + a + NZ) % NZ), dev(z=(z - a + NZ) % NZ))
    x_peer = [dev(x=(x + k) % NX) for k in range(1, NX)]
    y_peer = [dev(ylo=(ylo + k) % NYLO) for k in range(1, NYLO)]
    peers = [sibling, partner, *ahead, *x_peer, *y_peer]

    def remote(src, dst, ssem, rsem, to):
        return pltpu.make_async_remote_copy(
            src_ref=src, dst_ref=dst, send_sem=ssem, recv_sem=rsem, device_id=to, device_id_type=MESH
        )

    mine = pl.ds(pl.multiple_of(c * blk, blk), blk)
    other = pl.ds(pl.multiple_of((1 - c) * blk, blk), blk)

    x_rows = ROWS // NX
    y_rows = ROWS // N_REPLICA
    my_x = pl.ds(pl.multiple_of(x * x_rows, x_rows), x_rows)
    loads = [
        pltpu.make_async_copy(tokens.at[0], tok.at[0, mine], load_sem.at[0]),
        pltpu.make_async_copy(gate_w, gate_v, load_sem.at[1]),
        pltpu.make_async_copy(local_up.at[0], up_v, load_sem.at[2]),
        pltpu.make_async_copy(down_w, down_v, load_sem.at[3]),
        pltpu.make_async_copy(deltas.at[0, my_x], delta_v, load_sem.at[4]),
        pltpu.make_async_copy(outer_up, outer_v, load_sem.at[5]),
        pltpu.make_async_copy(momentum, mom_v, load_sem.at[6]),
    ]
    for load in loads:
        load.start()

    barrier = pltpu.get_barrier_semaphore()
    for peer in peers:
        pl.semaphore_signal(barrier, inc=1, device_id=peer, device_id_type=MESH)
    pl.semaphore_wait(barrier, len(peers))

    def slot_from(side, q, j):
        if j in (0, 4):
            return BASE[side][j]
        return BASE[side][j] + (1 - c if q == 0 else c)

    def slot_to(side, q, j):
        if j in (0, 4):
            return BASE[side][j]
        return BASE[side][j] + (c if q == 0 else 1 - c)

    def pass_on(side, q, j, src):
        s = slot_from(side, q, j + 1)
        return remote(src, tok.at[s, mine], ag_send.at[s], ag_recv.at[s], ahead[q])

    def to_sibling(s, src):
        return remote(src, tok.at[s, mine], ag_sib_send.at[s], ag_sib_recv.at[s], sibling)

    def y_tokens():
        s = BASE[PAR][0]
        return remote(tokens.at[0], tok.at[s, mine], yx_send.at[0], ag_recv.at[s], partner)

    def gathered(side, j):
        if j == 0:
            s = BASE[side][0]
            y_tokens().wait_recv()
            src = tok.at[s, mine]
            for q in (0, 1):
                pass_on(side, q, 0, src).start()
            to_sibling(s, src).start()
            return
        for q in (0, 1) if j < 4 else (0,):
            s = slot_from(side, q, j)
            src = tok.at[s, mine]
            remote(src, src, ag_send.at[s], ag_recv.at[s], ahead[q]).wait_recv()
            if j < (4 if q == 0 else 3):
                pass_on(side, q, j, src).start()
            to_sibling(s, src).start()

    def rs_index(side, q, j):
        return side * 7 + (4 - j if q == 0 else 4 + 3 - j)

    def rs_copy(side, q, j):
        i = rs_index(side, q, j)
        return remote(rs_out.at[i], rs_in.at[i], rs_send.at[i], rs_recv.at[i], ahead[q])

    def sib_copy(s):
        return remote(part.at[s, other], sib_part.at[s], ps_send.at[s], ps_recv.at[s], sibling)

    def my_terms(s):
        sib_copy(s).wait_recv()
        return part[s, mine, :].astype(F32) + sib_part[s].astype(F32)

    def reduce_send(side, q, j):
        total = my_terms(slot_to(side, q, j))
        if j < (4 if q == 0 else 3):
            before = rs_copy(side, q, j + 1)
            before.wait_recv()
            total = total + rs_in[rs_index(side, q, j + 1)].astype(F32)
        rs_out[rs_index(side, q, j)] = total.astype(BF16)
        rs_copy(side, q, j).start()

    def reduce_last(side):
        total = my_terms(BASE[side][0])
        for q in (0, 1):
            rs_copy(side, q, 1).wait_recv()
            total = total + rs_in[rs_index(side, q, 1)].astype(F32)
        return total

    def rows_of(k):
        return pl.ds(pl.multiple_of(k * y_rows, y_rows), y_rows)

    def x_leg(k):
        px = (x + k + 1) % NX
        rows = pl.ds(pl.multiple_of(px * x_rows, x_rows), x_rows)
        return remote(deltas.at[0, rows], x_in.at[k], o_send.at[k], o_recv.at[k], x_peer[k])

    def y_leg(k):
        py = (ylo + k + 1) % NYLO
        return remote(y_mid.at[rows_of(py)], y_sum_in.at[k], o_send.at[3 + k], o_recv.at[3 + k], y_peer[k])

    def y_gather(k):
        rows = rows_of(r)
        return remote(half_all.at[rows], half_all.at[rows], o_send.at[6 + k], o_recv.at[6 + k], y_peer[k])

    def x_gather(k):
        return remote(half_all.at[my_x], half_all.at[my_x], o_send.at[9 + k], o_recv.at[9 + k], x_peer[k])

    stores = [
        pltpu.make_async_copy(no_v, new_outer, store_sem.at[0]),
        pltpu.make_async_copy(nm_v, new_momentum, store_sem.at[1]),
        pltpu.make_async_copy(merged_v, merged_up.at[0], store_sem.at[2]),
        pltpu.make_async_copy(out_v, inner_out.at[0], store_sem.at[3]),
    ]

    def outer(stage):
        if stage == 1:
            for k in range(3):
                x_leg(k).start()
        elif stage == 2:
            loads[4].wait()
            total = delta_v[...].astype(F32)
            for k in range(3):
                x_leg(k).wait_recv()
                total = total + x_in[k].astype(F32)
            y_mid[...] = total.astype(BF16)
            for k in range(3):
                y_leg(k).start()
        elif stage == 3:
            loads[5].wait()
            loads[6].wait()
            total = y_mid[rows_of(ylo), :].astype(F32)
            for k in range(3):
                y_leg(k).wait_recv()
                total = total + y_sum_in[k].astype(F32)
            grad = total / N_REPLICA
            nm = momentum_coef * mom_v[...] + grad
            no = outer_v[...] - outer_rate * (grad + momentum_coef * nm)
            nm_v[...] = nm
            no_v[...] = no
            half_all[rows_of(r), :] = no.astype(BF16)
            for k in range(3):
                y_gather(k).start()
            stores[0].start()
            stores[1].start()
        elif stage == 4:
            for k in range(3):
                y_gather(k).wait_recv()
            for k in range(3):
                x_gather(k).start()
        else:
            for k in range(3):
                x_gather(k).wait_recv()
            merged = mix_weight * up_v[...].astype(F32) + (1.0 - mix_weight) * half_all[...].astype(F32)
            merged_v[...] = merged.astype(BF16)
            stores[2].start()

    for q in (0, 1):
        pass_on(OWN, q, 0, tokens.at[0]).start()
    y_tokens().start()
    to_sibling(0, tokens.at[0]).start()
    outer(1)
    for load in loads[:4]:
        load.wait()

    def compute(s):
        rows = tok[s]
        total = jnp.zeros((rows.shape[0], down_v.shape[1]), F32)
        width = gate_v.shape[1]
        for start in range(0, width, 256):
            cols = slice(start, min(start + 256, width))
            gate = jnp.dot(rows, gate_v[:, cols], preferred_element_type=F32)
            upper = jnp.dot(rows, up_v[:, cols], preferred_element_type=F32)
            hidden = ((gate + gate * jnp.tanh(0.5 * gate)) * upper).astype(BF16)
            total = total + jnp.dot(hidden, down_v[cols, :], preferred_element_type=F32)
        part[s] = (total * (0.5 * ROWS ** -0.5)).astype(BF16)

    def step(s, carry):
        for at in range(N_SLOT):
            if at in GATHER_AT or at in REDUCE_AT or at in OUTER_AT:

                @pl.when(s == at)
                def _():
                    for side, j in GATHER_AT.get(at, ()):
                        gathered(side, j)
                    for side, q, j in REDUCE_AT.get(at, ()):
                        reduce_send(side, q, j)
                    if at in OUTER_AT:
                        outer(OUTER_AT[at])

        half = tok.at[s, other]
        remote(half, half, ag_sib_send.at[s], ag_sib_recv.at[s], sibling).wait_recv()
        compute(s)
        sib_copy(s).start()
        return carry

    lax.fori_loop(0, N_SLOT, step, 0)

    reduce_send(PAR, 1, 3)
    reduce_send(PAR, 0, 4)
    reduce_send(OWN, 0, 3)
    reduce_send(OWN, 1, 1)
    reduce_send(PAR, 1, 2)
    reduce_send(PAR, 0, 3)
    reduce_send(OWN, 0, 2)
    reduce_send(PAR, 1, 1)
    reduce_send(PAR, 0, 2)
    reduce_send(OWN, 0, 1)
    outer(5)
    reduce_send(PAR, 0, 1)
    y_final = remote(rs_out.at[14], y_in, yx_send.at[1], yx_recv.at[0], partner)
    rs_out[14] = reduce_last(PAR).astype(BF16)
    y_final.start()
    own_sum[...] = reduce_last(OWN)
    y_final.wait_recv()
    out_v[...] = (own_sum[...] + y_in[...].astype(F32)).astype(BF16)
    stores[3].start()

    for side in (OWN, PAR):
        for j in range(0, 4):
            for q in (0, 1):
                if j < (4 if q == 0 else 3):
                    pass_on(side, q, j, tok.at[0, mine]).wait_send()
    y_tokens().wait_send()
    y_final.wait_send()
    for s in range(N_SLOT):
        to_sibling(s, tok.at[s, mine]).wait_send()
        sib_copy(s).wait_send()
    for side in (OWN, PAR):
        for j in range(1, 5):
            for q in (0, 1):
                if j < 4 or q == 0:
                    rs_copy(side, q, j).wait_send()
    for k in range(3):
        x_leg(k).wait_send()
        y_leg(k).wait_send()
        y_gather(k).wait_send()
        x_gather(k).wait_send()
    for store in stores:
        store.wait()


def body(tokens, gate_weight, down_weight, local_up, deltas, outer_up, momentum):
    blk, rows = tokens.shape[1:]
    width = gate_weight.shape[1]
    share = outer_up.shape[0]
    dma = pltpu.SemaphoreType.DMA
    return pl.pallas_call(
        kernel,
        out_shape=(
            jax.ShapeDtypeStruct(tokens.shape, BF16),
            jax.ShapeDtypeStruct(local_up.shape, BF16),
            jax.ShapeDtypeStruct(outer_up.shape, F32),
            jax.ShapeDtypeStruct(momentum.shape, F32),
        ),
        in_specs=[pl.BlockSpec(memory_space=pl.ANY)] * 7,
        out_specs=[pl.BlockSpec(memory_space=pl.ANY)] * 4,
        scratch_shapes=[
            pltpu.VMEM((N_SLOT, 2 * blk, rows), BF16),
            pltpu.VMEM(gate_weight.shape, BF16),
            pltpu.VMEM(local_up.shape[1:], BF16),
            pltpu.VMEM(down_weight.shape, BF16),
            pltpu.VMEM((ROWS // NX, width), BF16),
            pltpu.VMEM((share, width), F32),
            pltpu.VMEM((share, width), F32),
            pltpu.VMEM((N_SLOT, 2 * blk, rows), BF16),
            pltpu.VMEM((N_SLOT, blk, rows), BF16),
            pltpu.VMEM((14, blk, rows), BF16),
            pltpu.VMEM((15, blk, rows), BF16),
            pltpu.VMEM((blk, rows), BF16),
            pltpu.VMEM((blk, rows), F32),
            pltpu.VMEM((NX - 1, ROWS // NX, width), BF16),
            pltpu.VMEM((ROWS // NX, width), BF16),
            pltpu.VMEM((NYLO - 1, share, width), BF16),
            pltpu.VMEM((ROWS, width), BF16),
            pltpu.VMEM((ROWS, width), BF16),
            pltpu.VMEM((blk, rows), BF16),
            pltpu.VMEM((share, width), F32),
            pltpu.VMEM((share, width), F32),
            dma((7,)),
            dma((4,)),
            dma((N_SLOT,)),
            dma((N_SLOT,)),
            dma((N_SLOT,)),
            dma((N_SLOT,)),
            dma((N_SLOT,)),
            dma((N_SLOT,)),
            dma((14,)),
            dma((14,)),
            dma((2,)),
            dma((1,)),
            dma((12,)),
            dma((12,)),
        ],
        compiler_params=pltpu.CompilerParams(
            collective_id=0, has_side_effects=True, vmem_limit_bytes=48 * 1024 * 1024
        ),
        cost_estimate=pl.CostEstimate(flops=5_700_000_000, bytes_accessed=3_000_000, transcendentals=3_700_000),
    )(tokens, gate_weight, down_weight, local_up, deltas, outer_up, momentum)


def solution(mesh):
    placed = (
        P("replica", "fsdp", None),
        P(None, "fsdp"),
        P("fsdp", None),
        P("replica", None, "fsdp"),
        P("replica", None, "fsdp"),
        P("replica", "fsdp"),
        P("replica", "fsdp"),
    )
    return jax.shard_map(
        body,
        mesh=mesh,
        in_specs=placed,
        out_specs=(
            P("replica", "fsdp", None),
            P("replica", None, "fsdp"),
            P("replica", "fsdp"),
            P("replica", "fsdp"),
        ),
        check_vma=False,
    )
```

time: 269 us -> 71.1 us (0.26)
  waiting for transfers between devices: 192 us -> 0 us
  Pallas kernels: 0 us -> 60.8 us
  blocking collectives: 39.8 us -> 0 us
  matrix products: 18.4 us -> 0 us
  between operations: 15.5 us -> 0.66 us
  local copies, waits for them, and re-layouts: 0.02 us -> 9.18 us
    all_gather x1 -> x0, waiting for transfers between devices: 97.8 us -> none  [inner_pass(): rows = lax.all_gather(tokens, 'fsdp', axis=1, tiled=True)[0]]
    psum x1 -> x0, waiting for transfers between devices: 68.1 us -> none  [outer_sync(): lax.psum(summand.astype(jnp.bfloat16), 'replica').astype(jnp.float32)]
    pallas_call x0 -> x1, Pallas kernels: none -> 60.8 us  [body(): pl.pallas_call(kernel, out_shape=(jax.ShapeDtypeStruct(tokens.shape, BF16...]
    all_gather x1 -> x0, blocking collectives: 39.8 us -> none  [body(): lax.all_gather(new_outer.astype(jnp.bfloat16), 'replica', axis=0, tiled=T...]
    reduce_scatter x1 -> x0, waiting for transfers between devices: 25.3 us -> none  [inner_pass(): lax.psum_scatter(partial_terms.astype(jnp.bfloat16), 'fsdp', scatter_dime...]
    dot_general x2 -> x0, matrix products: 18.4 us -> none  [the longest x1 9.29 us: inner_pass(): gate = jnp.dot(rows, gate_weight, preferred_element_type=jnp.float32)]
    unnamed x10 -> x18, local copies, waits for them, and re-layouts: 0.02 us -> 9.18 us
  transfers between devices with their start and end apart: 3 -> 0, of which waited for: 3 -> 0; matrix products, arithmetic and copies ran while one was open for 8% -> 0% of each run, Pallas kernels for 0% -> 0%
where the time goes in v1:
time: 71.1 us; the launch traced here: 70.6 us
  Pallas kernels  60.8 us (86%)
  local copies, waits for them, and re-layouts  9.18 us (13%)
    pallas_call x1, Pallas kernels, body(): pl.pallas_call(kernel, out_shape=(jax.ShapeDtypeStruct(tokens.shape, BF16...  60.8 us
    unnamed x18, local copies, waits for them, and re-layouts  9.18 us

profile of v1, /device:TPU:2, one launch (start us, length us, event | category | flops | bytes accessed | tf_op | source)
XLA Modules:
  0.0 70.6 jit_solution(17906610000252647050)
XLA Ops:
  0.6 0.0 copy-start
  0.6 1.0 %copy-done = bf16[256,896]{1,0:T(8,128)(2,1)S(1)} copy-done((bf16[256,896]{1,0:T(8,128)(2,1)S(1)}, bf16[256,896]{1,0:T(8,128)(2,1)}, u32[]{:S(2)}) %copy-start) | copy-done | bytes 458776
  1.7 0.0 copy-start.1
  1.7 1.0 %copy-done.1 = bf16[896,256]{1,0:T(8,128)(2,1)S(1)} copy-done((bf16[896,256]{1,0:T(8,128)(2,1)S(1)}, bf16[896,256]{1,0:T(8,128)(2,1)}, u32[]{:S(2)}) %copy-start.1) | copy-done | bytes 458776
  2.7 0.0 copy-start.2
  2.7 1.0 %copy-done.2 = bf16[1,256,896]{2,1,0:T(8,128)(2,1)S(1)} copy-done((bf16[1,256,896]{2,1,0:T(8,128)(2,1)S(1)}, bf16[1,256,896]{2,1,0:T(8,128)(2,1)}, u32[]{:S(2)}) %copy-start.2) | copy-done | bytes 458776
  3.7 0.0 copy-start.3
  3.7 1.0 %copy-done.3 = bf16[1,256,896]{2,1,0:T(8,128)(2,1)S(1)} copy-done((bf16[1,256,896]{2,1,0:T(8,128)(2,1)S(1)}, bf16[1,256,896]{2,1,0:T(8,128)(2,1)}, u32[]{:S(2)}) %copy-start.3) | copy-done | bytes 458776
  4.7 0.0 copy-start.4
  4.7 0.8 %copy-done.4 = bf16[1,128,256]{2,1,0:T(8,128)(2,1)S(1)} copy-done((bf16[1,128,256]{2,1,0:T(8,128)(2,1)S(1)}, bf16[1,128,256]{2,1,0:T(8,128)(2,1)}, u32[]{:S(2)}) %copy-start.4) | copy-done | bytes 65560
  5.5 0.0 copy-start.5
  5.6 0.8 %copy-done.5 = f32[16,896]{1,0:T(8,128)S(1)} copy-done((f32[16,896]{1,0:T(8,128)S(1)}, f32[16,896]{1,0:T(8,128)}, u32[]{:S(2)}) %copy-start.5) | copy-done | bytes 57368
  6.4 0.0 copy-start.6
  6.4 0.8 %copy-done.6 = f32[16,896]{1,0:T(8,128)S(1)} copy-done((f32[16,896]{1,0:T(8,128)S(1)}, f32[16,896]{1,0:T(8,128)}, u32[]{:S(2)}) %copy-start.6) | copy-done | bytes 57368
  7.2 60.8 %shard_map.102 = (bf16[1,128,256]{2,1,0:T(8,128)(2,1)S(1)}, bf16[1,256,896]{2,1,0:T(8,128)(2,1)S(1)}, f32[16,896]{1,0:T(8,128)S(1)}, f32[16,896]{1,0:T(8,128)S(1)}) custom-call(bf16[1,128,256]{2,1,0:T(8,128)(2,1)S(1)} %copy-done.4, bf16[256,896]{1,0:T(8,128)(2,1)S(1)} %copy-done, bf16[896,256]{1,0:T(8,128)(2,1)S(1)} %copy-done.1, ...), custom_call_target="tpu_custom_call" | custom-call | flops 5699999744 | bytes 3000000 | tf_op jit(solution)/shard_map/pallas_call | solution.py:321
  68.0 0.6 copy.15
  68.6 0.8 %copy.16 = bf16[1,256,896]{2,1,0:T(8,128)(2,1)} copy(bf16[1,256,896]{2,1,0:T(8,128)(2,1)S(1)} %get-tuple-element.9) | data formatting | bytes 917504
  69.4 0.6 copy.17
  70.0 0.6 copy.18
Async XLA Ops:
  0.6 1.0 %copy-start = (bf16[256,896]{1,0:T(8,128)(2,1)S(1)}, bf16[256,896]{1,0:T(8,128)(2,1)}, u32[]{:S(2)}) copy-start(bf16[256,896]{1,0:T(8,128)(2,1)} %gate_w.1) | copy-start | bytes 1376260
  1.7 1.0 %copy-start.1 = (bf16[896,256]{1,0:T(8,128)(2,1)S(1)}, bf16[896,256]{1,0:T(8,128)(2,1)}, u32[]{:S(2)}) copy-start(bf16[896,256]{1,0:T(8,128)(2,1)} %down_w.1) | copy-start | bytes 1376260
  2.7 1.0 %copy-start.2 = (bf16[1,256,896]{2,1,0:T(8,128)(2,1)S(1)}, bf16[1,256,896]{2,1,0:T(8,128)(2,1)}, u32[]{:S(2)}) copy-start(bf16[1,256,896]{2,1,0:T(8,128)(2,1)} %local_up.1) | copy-start | bytes 1376260
  3.7 1.0 %copy-start.3 = (bf16[1,256,896]{2,1,0:T(8,128)(2,1)S(1)}, bf16[1,256,896]{2,1,0:T(8,128)(2,1)}, u32[]{:S(2)}) copy-start(bf16[1,256,896]{2,1,0:T(8,128)(2,1)} %deltas.1) | copy-start | bytes 1376260
  4.7 0.8 %copy-start.4 = (bf16[1,128,256]{2,1,0:T(8,128)(2,1)S(1)}, bf16[1,128,256]{2,1,0:T(8,128)(2,1)}, u32[]{:S(2)}) copy-start(bf16[1,128,256]{2,1,0:T(8,128)(2,1)} %tokens.1) | copy-start | bytes 196612
  5.5 0.8 %copy-start.5 = (f32[16,896]{1,0:T(8,128)S(1)}, f32[16,896]{1,0:T(8,128)}, u32[]{:S(2)}) copy-start(f32[16,896]{1,0:T(8,128)} %outer_up.1) | copy-start | bytes 172036
  6.4 0.8 %copy-start.6 = (f32[16,896]{1,0:T(8,128)S(1)}, f32[16,896]{1,0:T(8,128)}, u32[]{:S(2)}) copy-start(f32[16,896]{1,0:T(8,128)} %momentum.1) | copy-start | bytes 172036

commit v2 on v0

v2 whole, which is shorter than its diff:
```python
import jax
import jax.numpy as jnp
from jax import lax
from jax.experimental import pallas as pl
from jax.experimental.pallas import tpu as pltpu
from jax.sharding import PartitionSpec as P

MESH = pl.DeviceIdType.MESH
BF16, F32 = jnp.bfloat16, jnp.float32

NX, NYLO, NZ = 4, 4, 8
N_REPLICA = NX * NYLO
ROWS = 256

outer_rate = 0.7
momentum_coef = 0.9
mix_weight = 0.5

OWN, PAR = 0, 1
TREE = (
    ({1: 0, 2: 1, 3: 1, 4: 2}, {1: 0, 2: 1, 3: 2}),
    ({1: 0, 2: 0, 3: 2, 4: 2}, {1: 0, 2: 0, 3: 2}),
)
PAIRS = (
    ((0, 0, 0), (0, 0, 1)),
    ((0, 1, 1), (1, 0, 0)),
    ((0, 0, 2), (0, 1, 2)),
    ((1, 0, 1), (1, 0, 2)),
    ((1, 1, 1), (1, 1, 2)),
    ((0, 0, 3), (0, 1, 3)),
    ((1, 0, 4), (1, 0, 3)),
    ((0, 0, 4), (1, 1, 3)),
)
SLOT = {block: 2 * i + k for i, pair in enumerate(PAIRS) for k, block in enumerate(pair)}
N_SLOT = len(SLOT)

BEFORE = (
    (("g", 0, 0, 1),),
    (("g", 0, 1, 1),),
    (("y",),),
    (("g", 0, 0, 2),),
    (("g", 0, 0, 3), ("g", 0, 1, 2), ("o", 2)),
    (("g", 1, 0, 1),),
    (("g", 1, 0, 2),),
    (("g", 1, 1, 1),),
    (("r", 1, 0, 1), ("g", 1, 1, 2)),
    (),
    (("g", 0, 0, 4), ("r", 1, 1, 1), ("g", 0, 1, 3)),
    (("g", 1, 0, 3), ("o", 3)),
    (("r", 0, 0, 3), ("g", 1, 0, 4), ("r", 0, 1, 3)),
    (),
    (("g", 1, 1, 3), ("r", 1, 0, 4), ("r", 1, 0, 3)),
    (),
)
AFTER = (
    ("r", 1, 1, 3), ("r", 0, 0, 4), ("r", 0, 1, 2), ("o", 4), ("w", 0), ("r", 1, 0, 2), ("r", 1, 1, 2),
    ("r", 0, 0, 2), ("r", 0, 1, 1), ("w", 1), ("f", 1), ("r", 0, 0, 1), ("o", 5), ("w", 2), ("f", 0),
)


def kernel(
    tokens, gate_w, down_w, local_up, deltas, outer_up, momentum,
    out_v, merged_v, no_v, nm_v,
    tok, gate_v, up_v, down_v, delta_v, outer_v, mom_v,
    part, acc, rs_in, rs_out, y_out, y_in,
    x_in, y_mid, y_sum_in, half_all,
    load_sem, w_send, w_recv, ag_send, ag_recv, rs_send, rs_recv, y_send, y_recv, o_send, o_recv,
):
    r, f = lax.axis_index("replica"), lax.axis_index("fsdp")
    x, ylo = r // NYLO, r % NYLO
    z, yh, c = f // 4, (f // 2) % 2, f % 2
    a = 1 - 2 * c

    def dev(x=x, ylo=ylo, z=z, yh=yh, c=c):
        return (x * NYLO + ylo, z * 4 + yh * 2 + c)

    def along(q, d):
        return dev(z=(z + (a if q == 0 else -a) * d + NZ) % NZ)

    sibling = dev(c=1 - c)
    partner = dev(yh=1 - yh)
    x_peer = [dev(x=(x + k) % NX) for k in range(1, NX)]
    y_peer = [dev(ylo=(ylo + k) % NYLO) for k in range(1, NYLO)]
    steps = sorted({j - p for side in TREE for edges in side for j, p in edges.items()})
    peers = [sibling, partner, *x_peer, *y_peer] + [along(q, d) for d in steps for q in (0, 1)]

    def remote(src, dst, ssem, rsem, to):
        return pltpu.make_async_remote_copy(
            src_ref=src, dst_ref=dst, send_sem=ssem, recv_sem=rsem, device_id=to, device_id_type=MESH
        )

    x_rows = ROWS // NX
    y_rows = ROWS // N_REPLICA
    my_x = pl.ds(pl.multiple_of(x * x_rows, x_rows), x_rows)
    loads = [
        pltpu.make_async_copy(tokens.at[0], tok.at[SLOT[0, 0, 0]], load_sem.at[0]),
        pltpu.make_async_copy(gate_w, gate_v.at[0], load_sem.at[1]),
        pltpu.make_async_copy(local_up.at[0], up_v.at[0], load_sem.at[2]),
        pltpu.make_async_copy(down_w, down_v.at[0], load_sem.at[3]),
        pltpu.make_async_copy(deltas.at[0, my_x], delta_v, load_sem.at[4]),
        pltpu.make_async_copy(outer_up, outer_v, load_sem.at[5]),
        pltpu.make_async_copy(momentum, mom_v, load_sem.at[6]),
    ]
    for load in loads:
        load.start()

    barrier = pltpu.get_barrier_semaphore()
    for peer in peers:
        pl.semaphore_signal(barrier, inc=1, device_id=peer, device_id_type=MESH)
    pl.semaphore_wait(barrier, len(peers))

    def slot(side, q, j):
        return SLOT[side, 0 if j == 0 else q, j]

    def children(side, q, p):
        return [j for j, parent in TREE[side][q].items() if parent == p]

    def gather_copy(side, q, j, src=None):
        p, s = TREE[side][q][j], slot(side, q, j)
        src = tok.at[slot(side, q, p)] if src is None else src
        return remote(src, tok.at[s], ag_send.at[s], ag_recv.at[s], along(q, j - p))

    def y_tokens():
        s = SLOT[PAR, 0, 0]
        return remote(tokens.at[0], tok.at[s], y_send.at[0], ag_recv.at[s], partner)

    def reduce_copy(side, q, j):
        p, s = TREE[side][q][j], slot(side, q, j)
        src = rs_out if children(side, q, j) else part
        return remote(src.at[s], rs_in.at[s], rs_send.at[s], rs_recv.at[s], along(q, p - j))

    def sum_of(side, j, dirs):
        total = part[slot(side, dirs[0], j)].astype(F32)
        for q in dirs:
            for child in children(side, q, j):
                reduce_copy(side, q, child).wait_recv()
                total = total + rs_in[slot(side, q, child)].astype(F32)
        return total

    y_final = remote(y_out, y_in, y_send.at[1], y_recv.at[0], partner)

    def rows_of(k):
        return pl.ds(pl.multiple_of(k * y_rows, y_rows), y_rows)

    def x_leg(k):
        px = (x + k + 1) % NX
        rows = pl.ds(pl.multiple_of(px * x_rows, x_rows), x_rows)
        return remote(deltas.at[0, rows], x_in.at[k], o_send.at[k], o_recv.at[k], x_peer[k])

    def y_leg(k):
        py = (ylo + k + 1) % NYLO
        return remote(y_mid.at[rows_of(py)], y_sum_in.at[k], o_send.at[3 + k], o_recv.at[3 + k], y_peer[k])

    def y_gather(k):
        rows = rows_of(r)
        return remote(half_all.at[rows], half_all.at[rows], o_send.at[6 + k], o_recv.at[6 + k], y_peer[k])

    def x_gather(k):
        return remote(half_all.at[my_x], half_all.at[my_x], o_send.at[9 + k], o_recv.at[9 + k], x_peer[k])

    def outer(stage):
        if stage == 2:
            loads[4].wait()
            total = delta_v[...].astype(F32)
            for k in range(3):
                x_leg(k).wait_recv()
                total = total + x_in[k].astype(F32)
            y_mid[...] = total.astype(BF16)
            for k in range(3):
                y_leg(k).start()
        elif stage == 3:
            loads[5].wait()
            loads[6].wait()
            total = y_mid[rows_of(ylo), :].astype(F32)
            for k in range(3):
                y_leg(k).wait_recv()
                total = total + y_sum_in[k].astype(F32)
            grad = total / N_REPLICA
            nm = momentum_coef * mom_v[...] + grad
            no = outer_v[...] - outer_rate * (grad + momentum_coef * nm)
            nm_v[...] = nm
            no_v[...] = no
            half_all[rows_of(r), :] = no.astype(BF16)
            for k in range(3):
                y_gather(k).start()
        elif stage == 4:
            for k in range(3):
                y_gather(k).wait_recv()
            for k in range(3):
                x_gather(k).start()
        else:
            for k in range(3):
                x_gather(k).wait_recv()
            merged = mix_weight * up_v[0].astype(F32) + (1.0 - mix_weight) * half_all[...].astype(F32)
            merged_v[...] = merged.astype(BF16)

    weights = [
        remote(src, dst.at[1], w_send.at[k], w_recv.at[k], sibling)
        for k, (src, dst) in enumerate(((gate_w, gate_v), (local_up.at[0], up_v), (down_w, down_v)))
    ]

    def wait_sends(stage):
        if stage == 0:
            for weight in weights:
                weight.wait_send()
            y_tokens().wait_send()
            for side in (OWN, PAR):
                for q in (0, 1):
                    for j in TREE[side][q]:
                        gather_copy(side, q, j).wait_send()
            for k in range(3):
                x_leg(k).wait_send()
                y_leg(k).wait_send()
        elif stage == 1:
            for k in range(3):
                y_gather(k).wait_send()
        else:
            for k in range(3):
                x_gather(k).wait_send()
            for side in (OWN, PAR):
                for q in (0, 1):
                    for j in TREE[side][q]:
                        reduce_copy(side, q, j).wait_send()
            y_final.wait_send()

    def act(kind, *what):
        if kind == "g":
            side, q, j = what
            s = slot(side, q, j)
            gather_copy(side, q, j).wait_recv()
            for child in children(side, q, j):
                gather_copy(side, q, child).start()
        elif kind == "y":
            y_tokens().wait_recv()
            for q in (0, 1):
                for child in children(PAR, q, 0):
                    gather_copy(PAR, q, child).start()
        elif kind == "r":
            side, q, j = what
            if children(side, q, j):
                rs_out[slot(side, q, j)] = sum_of(side, j, (q,)).astype(BF16)
            reduce_copy(side, q, j).start()
        elif kind == "f":
            total = sum_of(what[0], 0, (0, 1))
            if what[0] == PAR:
                y_out[...] = total.astype(BF16)
                y_final.start()
            else:
                y_final.wait_recv()
                out_v[...] = (total + y_in[...].astype(F32)).astype(BF16)
        elif kind == "o":
            outer(what[0])
        else:
            wait_sends(what[0])

    for q in (0, 1):
        for child in children(OWN, q, 0):
            gather_copy(OWN, q, child, tokens.at[0]).start()
    y_tokens().start()
    for weight in weights:
        weight.start()
    for k in range(3):
        x_leg(k).start()
    for load in loads[:4]:
        load.wait()

    blk, width = tok.shape[1], gate_v.shape[2]

    def compute(i, h):
        rows = tok[pl.ds(2 * i, 2)].reshape(2 * blk, ROWS)
        total = jnp.zeros((2 * blk, ROWS), F32)
        for start in range(0, width, 256):
            cols = slice(start, min(start + 256, width))
            gate = jnp.dot(rows, gate_v[h, :, cols], preferred_element_type=F32)
            upper = jnp.dot(rows, up_v[h, :, cols], preferred_element_type=F32)
            hidden = ((gate + gate * jnp.tanh(0.5 * gate)) * upper).astype(BF16)
            total = total + jnp.dot(hidden, down_v[h, cols, :], preferred_element_type=F32)

        @pl.when(h == 0)
        def _():
            acc[...] = total

        @pl.when(h == 1)
        def _():
            both = (acc[...] + total) * (0.5 * ROWS ** -0.5)
            part[pl.ds(2 * i, 2)] = both.astype(BF16).reshape(2, blk, ROWS)

    def unit(u, carry):
        for at, todo in enumerate(BEFORE):
            if todo or at == 1:

                @pl.when(u == at)
                def _():
                    for what in todo:
                        act(*what)
                    if at == 1:
                        for weight in weights:
                            weight.wait_recv()

        compute(u // 2, u % 2)
        return carry

    lax.fori_loop(0, len(BEFORE), unit, 0)
    for what in AFTER:
        act(*what)


def store_kernel(*refs):
    n = (len(refs) - 1) // 2
    copies = [pltpu.make_async_copy(src, dst, refs[-1].at[k]) for k, (src, dst) in enumerate(zip(refs[:n], refs[n:-1]))]
    for copy in copies:
        copy.start()
    for copy in copies:
        copy.wait()


def body(tokens, gate_weight, down_weight, local_up, deltas, outer_up, momentum):
    blk, rows = tokens.shape[1:]
    width = gate_weight.shape[1]
    share = outer_up.shape[0]
    dma = pltpu.SemaphoreType.DMA
    outs = (
        ((blk, rows), BF16, tokens.shape),
        ((ROWS, width), BF16, local_up.shape),
        ((share, width), F32, outer_up.shape),
        ((share, width), F32, momentum.shape),
    )
    args = [
        pltpu.with_memory_space_constraint(arg, pltpu.HBM)
        for arg in (tokens, gate_weight, down_weight, local_up, deltas, outer_up, momentum)
    ]
    held = pl.pallas_call(
        kernel,
        out_shape=tuple(pltpu.VMEM(shape, kind) for shape, kind, _ in outs),
        in_specs=[pl.BlockSpec(memory_space=pltpu.HBM)] * 7,
        out_specs=[pl.BlockSpec(memory_space=pltpu.VMEM)] * 4,
        scratch_shapes=[
            pltpu.VMEM((N_SLOT, blk, rows), BF16),
            pltpu.VMEM((2, ROWS, width), BF16),
            pltpu.VMEM((2, ROWS, width), BF16),
            pltpu.VMEM((2, width, ROWS), BF16),
            pltpu.VMEM((ROWS // NX, width), BF16),
            pltpu.VMEM((share, width), F32),
            pltpu.VMEM((share, width), F32),
            pltpu.VMEM((N_SLOT, blk, rows), BF16),
            pltpu.VMEM((2 * blk, rows), F32),
            pltpu.VMEM((N_SLOT, blk, rows), BF16),
            pltpu.VMEM((N_SLOT, blk, rows), BF16),
            pltpu.VMEM((blk, rows), BF16),
            pltpu.VMEM((blk, rows), BF16),
            pltpu.VMEM((NX - 1, ROWS // NX, width), BF16),
            pltpu.VMEM((ROWS // NX, width), BF16),
            pltpu.VMEM((NYLO - 1, share, width), BF16),
            pltpu.VMEM((ROWS, width), BF16),
            dma((7,)),
            dma((3,)),
            dma((3,)),
            dma((N_SLOT,)),
            dma((N_SLOT,)),
            dma((N_SLOT,)),
            dma((N_SLOT,)),
            dma((2,)),
            dma((1,)),
            dma((12,)),
            dma((12,)),
        ],
        compiler_params=pltpu.CompilerParams(
            collective_id=0, has_side_effects=True, vmem_limit_bytes=32 * 1024 * 1024
        ),
        cost_estimate=pl.CostEstimate(flops=5_700_000_000, bytes_accessed=3_000_000, transcendentals=3_700_000),
    )(*args)
    inner_out, merged_up, new_outer, new_momentum = pl.pallas_call(
        store_kernel,
        out_shape=tuple(jax.ShapeDtypeStruct(shape, kind) for shape, kind, _ in outs),
        in_specs=[pl.BlockSpec(memory_space=pltpu.VMEM)] * 4,
        out_specs=[pl.BlockSpec(memory_space=pl.ANY)] * 4,
        scratch_shapes=[dma((4,))],
    )(*held)
    return inner_out[None], merged_up[None], new_outer, new_momentum


def solution(mesh):
    placed = (
        P("replica", "fsdp", None),
        P(None, "fsdp"),
        P("fsdp", None),
        P("replica", None, "fsdp"),
        P("replica", None, "fsdp"),
        P("replica", "fsdp"),
        P("replica", "fsdp"),
    )
    return jax.shard_map(
        body,
        mesh=mesh,
        in_specs=placed,
        out_specs=(
            P("replica", "fsdp", None),
            P("replica", None, "fsdp"),
            P("replica", "fsdp"),
            P("replica", "fsdp"),
        ),
        check_vma=False,
    )
```

time: 269 us -> 59.3 us (0.22)
  waiting for transfers between devices: 192 us -> 0 us
  Pallas kernels: 0 us -> 55.9 us
  blocking collectives: 39.8 us -> 0 us
  matrix products: 18.4 us -> 0 us
  between operations: 15.5 us -> 0.65 us
    all_gather x1 -> x0, waiting for transfers between devices: 97.8 us -> none  [inner_pass(): rows = lax.all_gather(tokens, 'fsdp', axis=1, tiled=True)[0]]
    psum x1 -> x0, waiting for transfers between devices: 68.1 us -> none  [outer_sync(): lax.psum(summand.astype(jnp.bfloat16), 'replica').astype(jnp.float32)]
    pallas_call x0 -> x2, Pallas kernels: none -> 55.9 us  [the longest x1 54 us: body(): pl.pallas_call(kernel, out_shape=tuple((pltpu.VMEM(shape, kind) for shape...]
    all_gather x1 -> x0, blocking collectives: 39.8 us -> none  [body(): lax.all_gather(new_outer.astype(jnp.bfloat16), 'replica', axis=0, tiled=T...]
    reduce_scatter x1 -> x0, waiting for transfers between devices: 25.3 us -> none  [inner_pass(): lax.psum_scatter(partial_terms.astype(jnp.bfloat16), 'fsdp', scatter_dime...]
    dot_general x2 -> x0, matrix products: 18.4 us -> none  [the longest x1 9.29 us: inner_pass(): gate = jnp.dot(rows, gate_weight, preferred_element_type=jnp.float32)]
  transfers between devices with their start and end apart: 3 -> 0, of which waited for: 3 -> 0; matrix products, arithmetic and copies ran while one was open for 8% -> 0% of each run, Pallas kernels for 0% -> 0%
where the time goes in v2:
time: 59.3 us; the launch traced here: 59.2 us
  Pallas kernels  55.9 us (94%)
  local copies, waits for them, and re-layouts  2.61 us (4%)
  between operations  0.65 us (1%)
    pallas_call x1, Pallas kernels, body(): pl.pallas_call(kernel, out_shape=tuple((pltpu.VMEM(shape, kind) for shape...  54 us
    unnamed x8, local copies, waits for them, and re-layouts  2.61 us
    pallas_call x1, Pallas kernels, body(): pl.pallas_call(store_kernel, out_shape=tuple((jax.ShapeDtypeStruct(shape,...  1.87 us

profile of v2, /device:TPU:2, one launch (start us, length us, event | category | flops | bytes accessed | tf_op | source)
XLA Modules:
  0.0 59.2 jit_solution(13343597199147388543)
XLA Ops:
  0.6 54.0 %shard_map.102 = (bf16[128,256]{1,0:T(8,128)(2,1)S(1)}, bf16[256,896]{1,0:T(8,128)(2,1)S(1)}, f32[16,896]{1,0:T(8,128)S(1)}, f32[16,896]{1,0:T(8,128)S(1)}) custom-call(bf16[1,128,256]{2,1,0:T(8,128)(2,1)} %tokens.1, bf16[256,896]{1,0:T(8,128)(2,1)} %gate_w.1, bf16[896,256]{1,0:T(8,128)(2,1)} %down_w.1, bf16[1,256,896]{2,1,0:T(8,128)(2,1)} %local_up.1, ...), custom_call_target="tpu_custom_call" | custom-call | flops 5699999744 | bytes 3000000 | tf_op jit(solution)/shard_map/pallas_call | solution.py:332
  54.7 0.0 copy-start
  54.7 0.8 %copy-done = bf16[256,896]{1,0:T(8,128)(2,1)} copy-done((bf16[256,896]{1,0:T(8,128)(2,1)}, bf16[256,896]{1,0:T(8,128)(2,1)S(1)}, u32[]{:S(2)}) %copy-start) | copy-done | bytes 458776
  55.4 0.0 copy-start.1
  55.4 0.6 %copy-done.1 = bf16[128,256]{1,0:T(8,128)(2,1)} copy-done((bf16[128,256]{1,0:T(8,128)(2,1)}, bf16[128,256]{1,0:T(8,128)(2,1)S(1)}, u32[]{:S(2)}) %copy-start.1) | copy-done | bytes 65560
  56.1 0.0 copy-start.2
  56.1 0.6 %copy-done.2 = f32[16,896]{1,0:T(8,128)} copy-done((f32[16,896]{1,0:T(8,128)}, f32[16,896]{1,0:T(8,128)S(1)}, u32[]{:S(2)}) %copy-start.2) | copy-done | bytes 57368
  56.7 0.0 copy-start.3
  56.7 0.6 %copy-done.3 = f32[16,896]{1,0:T(8,128)} copy-done((f32[16,896]{1,0:T(8,128)}, f32[16,896]{1,0:T(8,128)S(1)}, u32[]{:S(2)}) %copy-start.3) | copy-done | bytes 57368
  57.3 1.9 %shard_map.103 = (bf16[128,256]{1,0:T(8,128)(2,1)}, bf16[256,896]{1,0:T(8,128)(2,1)}, f32[16,896]{1,0:T(8,128)}, f32[16,896]{1,0:T(8,128)}) custom-call(bf16[128,256]{1,0:T(8,128)(2,1)} %copy-done.1, bf16[256,896]{1,0:T(8,128)(2,1)} %copy-done, f32[16,896]{1,0:T(8,128)} %copy-done.2, f32[16,896]{1,0:T(8,128)} %copy-done.3), custom_call_target="tpu_custom_call" | custom-call | tf_op jit(solution)/shard_map/pallas_call | solution.py:372
Async XLA Ops:
  54.7 0.8 %copy-start = (bf16[256,896]{1,0:T(8,128)(2,1)}, bf16[256,896]{1,0:T(8,128)(2,1)S(1)}, u32[]{:S(2)}) copy-start(bf16[256,896]{1,0:T(8,128)(2,1)S(1)} %get-tuple-element.13.refs_1_) | copy-start | bytes 1376260
  55.4 0.6 %copy-start.1 = (bf16[128,256]{1,0:T(8,128)(2,1)}, bf16[128,256]{1,0:T(8,128)(2,1)S(1)}, u32[]{:S(2)}) copy-start(bf16[128,256]{1,0:T(8,128)(2,1)S(1)} %get-tuple-element.12.refs_0_) | copy-start | bytes 196612
  56.1 0.6 %copy-start.2 = (f32[16,896]{1,0:T(8,128)}, f32[16,896]{1,0:T(8,128)S(1)}, u32[]{:S(2)}) copy-start(f32[16,896]{1,0:T(8,128)S(1)} %get-tuple-element.14.refs_2_) | copy-start | bytes 172036
  56.7 0.6 %copy-start.3 = (f32[16,896]{1,0:T(8,128)}, f32[16,896]{1,0:T(8,128)S(1)}, u32[]{:S(2)}) copy-start(f32[16,896]{1,0:T(8,128)S(1)} %get-tuple-element.15.refs_3_) | copy-start | bytes 172036

commit v3 on v2

--- a/solution.py
+++ b/solution.py
@@ -375,7 +375,8 @@
         in_specs=[pl.BlockSpec(memory_space=pltpu.VMEM)] * 4,
         out_specs=[pl.BlockSpec(memory_space=pl.ANY)] * 4,
         scratch_shapes=[dma((4,))],
-    )(*held)
+        compiler_params=pltpu.CompilerParams(vmem_limit_bytes=1024 * 1024),
+    )(*[pltpu.with_memory_space_constraint(part, pltpu.VMEM) for part in held])
     return inner_out[None], merged_up[None], new_outer, new_momentum
 
 

time: 59.3 us -> 55.7 us (0.939)
  local copies, waits for them, and re-layouts: 2.61 us -> 0 us
  Pallas kernels: 55.9 us -> 54.9 us
    unnamed x8 -> x0, local copies, waits for them, and re-layouts: 2.61 us -> none
    pallas_call x1, Pallas kernels: 1.87 us -> 0.85 us  [body(): pl.pallas_call(store_kernel, out_shape=tuple((jax.ShapeDtypeStruct(shape,...]
where the time goes in v3:
time: 55.7 us; the launch traced here: 55.5 us
  Pallas kernels  54.9 us (99%)
  between operations  0.64 us (1%)
    pallas_call x1, Pallas kernels, body(): pl.pallas_call(kernel, out_shape=tuple((pltpu.VMEM(shape, kind) for shape...  54 us

profile of v3, /device:TPU:2, one launch (start us, length us, event | category | flops | bytes accessed | tf_op | source)
XLA Modules:
  0.0 55.5 jit_solution(783682668902987992)
XLA Ops:
  0.6 54.0 %shard_map.102 = (bf16[128,256]{1,0:T(8,128)(2,1)S(1)}, bf16[256,896]{1,0:T(8,128)(2,1)S(1)}, f32[16,896]{1,0:T(8,128)S(1)}, f32[16,896]{1,0:T(8,128)S(1)}) custom-call(bf16[1,128,256]{2,1,0:T(8,128)(2,1)} %tokens.1, bf16[256,896]{1,0:T(8,128)(2,1)} %gate_w.1, bf16[896,256]{1,0:T(8,128)(2,1)} %down_w.1, bf16[1,256,896]{2,1,0:T(8,128)(2,1)} %local_up.1, ...), custom_call_target="tpu_custom_call" | custom-call | flops 5699999744 | bytes 3000000 | tf_op jit(solution)/shard_map/pallas_call | solution.py:332
  54.7 0.9 %shard_map.103 = (bf16[128,256]{1,0:T(8,128)(2,1)}, bf16[256,896]{1,0:T(8,128)(2,1)}, f32[16,896]{1,0:T(8,128)}, f32[16,896]{1,0:T(8,128)}) custom-call(bf16[128,256]{1,0:T(8,128)(2,1)S(1)} %get-tuple-element.12.refs_0_, bf16[256,896]{1,0:T(8,128)(2,1)S(1)} %get-tuple-element.13.refs_1_, f32[16,896]{1,0:T(8,128)S(1)} %get-tuple-element.14.refs_2_, ...), custom_call_target="tpu_custom_call" | custom-call | tf_op jit(solution)/shard_map/pallas_call | solution.py:372

commit v4 on v3

--- a/solution.py
+++ b/solution.py
@@ -18,15 +18,15 @@
 
 OWN, PAR = 0, 1
 TREE = (
-    ({1: 0, 2: 1, 3: 1, 4: 2}, {1: 0, 2: 1, 3: 2}),
+    ({1: 0, 2: 1, 3: 2, 4: 2}, {1: 0, 2: 1, 3: 2}),
     ({1: 0, 2: 0, 3: 2, 4: 2}, {1: 0, 2: 0, 3: 2}),
 )
 PAIRS = (
     ((0, 0, 0), (0, 0, 1)),
     ((0, 1, 1), (1, 0, 0)),
     ((0, 0, 2), (0, 1, 2)),
-    ((1, 0, 1), (1, 0, 2)),
-    ((1, 1, 1), (1, 1, 2)),
+    ((1, 0, 1), (1, 1, 1)),
+    ((1, 0, 2), (1, 1, 2)),
     ((0, 0, 3), (0, 1, 3)),
     ((1, 0, 4), (1, 0, 3)),
     ((0, 0, 4), (1, 1, 3)),
@@ -39,22 +39,35 @@
     (("g", 0, 1, 1),),
     (("y",),),
     (("g", 0, 0, 2),),
-    (("g", 0, 0, 3), ("g", 0, 1, 2), ("o", 2)),
-    (("g", 1, 0, 1),),
-    (("g", 1, 0, 2),),
-    (("g", 1, 1, 1),),
-    (("r", 1, 0, 1), ("g", 1, 1, 2)),
+    (("g", 0, 1, 2),),
     (),
-    (("g", 0, 0, 4), ("r", 1, 1, 1), ("g", 0, 1, 3)),
-    (("g", 1, 0, 3), ("o", 3)),
-    (("r", 0, 0, 3), ("g", 1, 0, 4), ("r", 0, 1, 3)),
+    (("g", 1, 0, 1), ("o", 2), ("g", 1, 0, 2), ("g", 1, 1, 1),),
     (),
-    (("g", 1, 1, 3), ("r", 1, 0, 4), ("r", 1, 0, 3)),
+    (("g", 1, 1, 2), ("r", 1, 0, 1), ("r", 1, 1, 1),),
+    (("g", 0, 0, 3),),
+    (("g", 0, 0, 4), ("g", 0, 1, 3),),
+    (("g", 1, 0, 3), ("o", 3),),
+    (("r", 0, 0, 3), ("g", 1, 0, 4), ("r", 0, 1, 3),),
+    (("g", 1, 1, 3),),
+    (("r", 1, 0, 4), ("r", 1, 0, 3),),
     (),
 )
 AFTER = (
-    ("r", 1, 1, 3), ("r", 0, 0, 4), ("r", 0, 1, 2), ("o", 4), ("w", 0), ("r", 1, 0, 2), ("r", 1, 1, 2),
-    ("r", 0, 0, 2), ("r", 0, 1, 1), ("w", 1), ("f", 1), ("r", 0, 0, 1), ("o", 5), ("w", 2), ("f", 0),
+    ("r", 1, 1, 3),
+    ("r", 0, 0, 4),
+    ("r", 0, 1, 2),
+    ("o", 4),
+    ("r", 1, 0, 2),
+    ("w", 0),
+    ("r", 1, 1, 2),
+    ("r", 0, 0, 2),
+    ("r", 0, 1, 1),
+    ("w", 1),
+    ("f", 1),
+    ("r", 0, 0, 1),
+    ("o", 5),
+    ("w", 2),
+    ("f", 0),
 )
 
 
@@ -82,7 +95,7 @@
     x_peer = [dev(x=(x + k) % NX) for k in range(1, NX)]
     y_peer = [dev(ylo=(ylo + k) % NYLO) for k in range(1, NYLO)]
     steps = sorted({j - p for side in TREE for edges in side for j, p in edges.items()})
-    peers = [sibling, partner, *x_peer, *y_peer] + [along(q, d) for d in steps for q in (0, 1)]
+    peers = [along(q, d) for d in steps for q in (0, 1)] + [partner, sibling, *x_peer, *y_peer]
 
     def remote(src, dst, ssem, rsem, to):
         return pltpu.make_async_remote_copy(
@@ -101,12 +114,11 @@
         pltpu.make_async_copy(outer_up, outer_v, load_sem.at[5]),
         pltpu.make_async_copy(momentum, mom_v, load_sem.at[6]),
     ]
-    for load in loads:
-        load.start()
-
     barrier = pltpu.get_barrier_semaphore()
     for peer in peers:
         pl.semaphore_signal(barrier, inc=1, device_id=peer, device_id_type=MESH)
+    for load in loads:
+        load.start()
     pl.semaphore_wait(barrier, len(peers))
 
     def slot(side, q, j):
@@ -129,13 +141,25 @@
         src = rs_out if children(side, q, j) else part
         return remote(src.at[s], rs_in.at[s], rs_send.at[s], rs_recv.at[s], along(q, p - j))
 
-    def sum_of(side, j, dirs):
-        total = part[slot(side, dirs[0], j)].astype(F32)
-        for q in dirs:
-            for child in children(side, q, j):
-                reduce_copy(side, q, child).wait_recv()
-                total = total + rs_in[slot(side, q, child)].astype(F32)
-        return total
+    def in_rows(n, size, work):
+        def turn(i, carry):
+            work(pl.ds(pl.multiple_of(i * size, size), size))
+            return carry
+
+        lax.fori_loop(0, n, turn, 0)
+
+    def sum_into(side, j, dirs, store):
+        held = [(q, child) for q in dirs for child in children(side, q, j)]
+        for q, child in held:
+            reduce_copy(side, q, child).wait_recv()
+
+        def work(rows):
+            total = part[slot(side, dirs[0], j), rows, :].astype(F32)
+            for q, child in held:
+                total = total + rs_in[slot(side, q, child), rows, :].astype(F32)
+            store(rows, total)
+
+        in_rows(4, tok.shape[1] // 4, work)
 
     y_final = remote(y_out, y_in, y_send.at[1], y_recv.at[0], partner)
 
@@ -161,11 +185,16 @@
     def outer(stage):
         if stage == 2:
             loads[4].wait()
-            total = delta_v[...].astype(F32)
             for k in range(3):
                 x_leg(k).wait_recv()
-                total = total + x_in[k].astype(F32)
-            y_mid[...] = total.astype(BF16)
+
+            def work(rows):
+                total = delta_v[rows, :].astype(F32)
+                for k in range(3):
+                    total = total + x_in[k, rows, :].astype(F32)
+                y_mid[rows, :] = total.astype(BF16)
+
+            in_rows(4, x_rows // 4, work)
             for k in range(3):
                 y_leg(k).start()
         elif stage == 3:
@@ -191,23 +220,35 @@
         else:
             for k in range(3):
                 x_gather(k).wait_recv()
-            merged = mix_weight * up_v[0].astype(F32) + (1.0 - mix_weight) * half_all[...].astype(F32)
-            merged_v[...] = merged.astype(BF16)
+
+            def work(rows):
+                merged = mix_weight * up_v[0, rows, :].astype(F32) + (1.0 - mix_weight) * half_all[rows, :].astype(F32)
+                merged_v[rows, :] = merged.astype(BF16)
+
+            in_rows(16, ROWS // 16, work)
 
     weights = [
         remote(src, dst.at[1], w_send.at[k], w_recv.at[k], sibling)
         for k, (src, dst) in enumerate(((gate_w, gate_v), (local_up.at[0], up_v), (down_w, down_v)))
     ]
+
+    def sent_all(held, sem):
+        first, second = sorted((SLOT[OWN, 0, 0], SLOT[PAR, 0, 0]))
+
+        def turn(s, carry):
+            remote(held.at[s], held.at[s], sem.at[s], sem.at[s], partner).wait_send()
+            return carry
+
+        for low, high in ((0, first), (first + 1, second), (second + 1, N_SLOT)):
+            if low < high:
+                lax.fori_loop(low, high, turn, 0)
 
     def wait_sends(stage):
         if stage == 0:
             for weight in weights:
                 weight.wait_send()
             y_tokens().wait_send()
-            for side in (OWN, PAR):
-                for q in (0, 1):
-                    for j in TREE[side][q]:
-                        gather_copy(side, q, j).wait_send()
+            sent_all(tok, ag_send)
             for k in range(3):
                 x_leg(k).wait_send()
                 y_leg(k).wait_send()
@@ -217,10 +258,7 @@
         else:
             for k in range(3):
                 x_gather(k).wait_send()
-            for side in (OWN, PAR):
-                for q in (0, 1):
-                    for j in TREE[side][q]:
-                        reduce_copy(side, q, j).wait_send()
+            sent_all(part, rs_send)
             y_final.wait_send()
 
     def act(kind, *what):
@@ -238,16 +276,28 @@
         elif kind == "r":
             side, q, j = what
             if children(side, q, j):
-                rs_out[slot(side, q, j)] = sum_of(side, j, (q,)).astype(BF16)
+
+
+                def store(rows, total):
+                    rs_out[slot(side, q, j), rows, :] = total.astype(BF16)
+
+                sum_into(side, j, (q,), store)
             reduce_copy(side, q, j).start()
         elif kind == "f":
-            total = sum_of(what[0], 0, (0, 1))
             if what[0] == PAR:
-                y_out[...] = total.astype(BF16)
+
+                def store(rows, total):
+                    y_out[rows, :] = total.astype(BF16)
+
+                sum_into(PAR, 0, (0, 1), store)
                 y_final.start()
             else:
+
+                def store(rows, total):
+                    out_v[rows, :] = (total + y_in[rows, :].astype(F32)).astype(BF16)
+
                 y_final.wait_recv()
-                out_v[...] = (total + y_in[...].astype(F32)).astype(BF16)
+                sum_into(OWN, 0, (0, 1), store)
         elif kind == "o":
             outer(what[0])
         else:
@@ -285,18 +335,22 @@
             both = (acc[...] + total) * (0.5 * ROWS ** -0.5)
             part[pl.ds(2 * i, 2)] = both.astype(BF16).reshape(2, blk, ROWS)
 
+    def prepare(at):
+        for what in BEFORE[at]:
+            act(*what)
+        if at == 1:
+            for weight in weights:
+                weight.wait_recv()
+
+    def dispatch(u, low, high):
+        if high - low == 1:
+            prepare(low)
+            return
+        middle = (low + high) // 2
+        lax.cond(u < middle, lambda: dispatch(u, low, middle), lambda: dispatch(u, middle, high))
+
     def unit(u, carry):
-        for at, todo in enumerate(BEFORE):
-            if todo or at == 1:
-
-                @pl.when(u == at)
-                def _():
-                    for what in todo:
-                        act(*what)
-                    if at == 1:
-                        for weight in weights:
-                            weight.wait_recv()
-
+        dispatch(u, 0, len(BEFORE))
         compute(u // 2, u % 2)
         return carry
 

time: 55.7 us -> 53.3 us (0.957)
  the two profiles are of different devices: /device:TPU:2 before, /device:TPU:66 now
where the time goes in v4:
time: 53.3 us; the launch traced here: 53.2 us
  Pallas kernels  52.5 us (98%)
  between operations  0.64 us (1%)
    pallas_call x1, Pallas kernels, body(): pl.pallas_call(kernel, out_shape=tuple((pltpu.VMEM(shape, kind) for shape...  51.7 us

profile of v4, /device:TPU:66, one launch (start us, length us, event | category | flops | bytes accessed | tf_op | source)
XLA Modules:
  0.0 53.2 jit_solution(12339569613557157153)
XLA Ops:
  0.6 51.7 %shard_map.102 = (bf16[128,256]{1,0:T(8,128)(2,1)S(1)}, bf16[256,896]{1,0:T(8,128)(2,1)S(1)}, f32[16,896]{1,0:T(8,128)S(1)}, f32[16,896]{1,0:T(8,128)S(1)}) custom-call(bf16[1,128,256]{2,1,0:T(8,128)(2,1)} %tokens.1, bf16[256,896]{1,0:T(8,128)(2,1)} %gate_w.1, bf16[896,256]{1,0:T(8,128)(2,1)} %down_w.1, bf16[1,256,896]{2,1,0:T(8,128)(2,1)} %local_up.1, ...), custom_call_target="tpu_custom_call" | custom-call | flops 5699999744 | bytes 3000000 | tf_op jit(solution)/shard_map/pallas_call | solution.py:386
  52.3 0.9 %shard_map.103 = (bf16[128,256]{1,0:T(8,128)(2,1)}, bf16[256,896]{1,0:T(8,128)(2,1)}, f32[16,896]{1,0:T(8,128)}, f32[16,896]{1,0:T(8,128)}) custom-call(bf16[128,256]{1,0:T(8,128)(2,1)S(1)} %get-tuple-element.12.refs_0_, bf16[256,896]{1,0:T(8,128)(2,1)S(1)} %get-tuple-element.13.refs_1_, f32[16,896]{1,0:T(8,128)S(1)} %get-tuple-element.14.refs_2_, ...), custom_call_target="tpu_custom_call" | custom-call | tf_op jit(solution)/shard_map/pallas_call | solution.py:426

commit v5 on v4

--- a/solution.py
+++ b/solution.py
@@ -17,57 +17,123 @@
 mix_weight = 0.5
 
 OWN, PAR = 0, 1
+
+
+def hop(p, e):
+    d = (e - p) % NZ
+    return d - NZ if d > NZ // 2 else d
+
+
 TREE = (
-    ({1: 0, 2: 1, 3: 2, 4: 2}, {1: 0, 2: 1, 3: 2}),
-    ({1: 0, 2: 0, 3: 2, 4: 2}, {1: 0, 2: 0, 3: 2}),
+    (
+        {1: 0, 2: 1, 3: 2, 4: 2, -1: 0, -2: -1, -3: -2},
+        {1: 0, 2: 0, 3: 2, 4: 2, -1: 0, -2: 0, -3: -2},
+    ),
+    (
+        {1: 0, 2: 1, 3: 2, 4: 3, -1: 0, -2: -1, -3: -2},
+        {1: 0, 2: 0, 3: 2, 4: 2, -1: 0, -2: 0, -3: -2},
+    ),
 )
 PAIRS = (
-    ((0, 0, 0), (0, 0, 1)),
-    ((0, 1, 1), (1, 0, 0)),
-    ((0, 0, 2), (0, 1, 2)),
-    ((1, 0, 1), (1, 1, 1)),
-    ((1, 0, 2), (1, 1, 2)),
-    ((0, 0, 3), (0, 1, 3)),
-    ((1, 0, 4), (1, 0, 3)),
-    ((0, 0, 4), (1, 1, 3)),
+    (
+        ((0, 0), (0, 1)),
+        ((0, -1), (1, 0)),
+        ((0, 2), (0, -2)),
+        ((1, 1), (1, -1)),
+        ((1, 2), (1, -2)),
+        ((0, 3), (0, -3)),
+        ((1, 4), (1, 3)),
+        ((0, 4), (1, -3)),
+    ),
+    (
+        ((0, 0), (0, 1)),
+        ((0, -1), (1, 0)),
+        ((0, 2), (0, -2)),
+        ((1, 1), (1, -1)),
+        ((1, 2), (1, -2)),
+        ((0, 3), (0, -3)),
+        ((1, 4), (1, 3)),
+        ((0, 4), (1, -3)),
+    ),
 )
-SLOT = {block: 2 * i + k for i, pair in enumerate(PAIRS) for k, block in enumerate(pair)}
-N_SLOT = len(SLOT)
+SLOT = [{block: 2 * i + k for i, pair in enumerate(pairs) for k, block in enumerate(pair)} for pairs in PAIRS]
+N_SLOT = len(SLOT[0])
 
 BEFORE = (
-    (("g", 0, 0, 1),),
-    (("g", 0, 1, 1),),
-    (("y",),),
-    (("g", 0, 0, 2),),
-    (("g", 0, 1, 2),),
-    (),
-    (("g", 1, 0, 1), ("o", 2), ("g", 1, 0, 2), ("g", 1, 1, 1),),
-    (),
-    (("g", 1, 1, 2), ("r", 1, 0, 1), ("r", 1, 1, 1),),
-    (("g", 0, 0, 3),),
-    (("g", 0, 0, 4), ("g", 0, 1, 3),),
-    (("g", 1, 0, 3), ("o", 3),),
-    (("r", 0, 0, 3), ("g", 1, 0, 4), ("r", 0, 1, 3),),
-    (("g", 1, 1, 3),),
-    (("r", 1, 0, 4), ("r", 1, 0, 3),),
-    (),
+    (
+        (("g", 0, 1),),
+        (("g", 0, -1),),
+        (("g", 1, 0),),
+        (("g", 0, 2),),
+        (("g", 0, -2),),
+        (),
+        (("g", 1, 1), ("o", 2), ("g", 1, 2), ("g", 1, -1),),
+        (),
+        (("g", 1, -2), ("r", 1, 1), ("r", 1, -1),),
+        (("g", 0, 3),),
+        (("g", 0, 4), ("g", 0, -3),),
+        (("g", 1, 3), ("o", 3),),
+        (("r", 0, 3), ("g", 1, 4), ("r", 0, -3),),
+        (("g", 1, -3),),
+        (("r", 1, 4), ("r", 1, 3),),
+        (),
+    ),
+    (
+        (("g", 0, 1), ("g", 0, -1), ("g", 1, 0),),
+        (),
+        (),
+        (),
+        (("g", 0, 2), ("g", 0, -2),),
+        (("o", 2),),
+        (("g", 1, 1), ("g", 1, 2), ("g", 1, -1),),
+        (),
+        (("g", 1, -2),),
+        (),
+        (("g", 0, 3), ("r", 1, 1), ("r", 1, -1), ("g", 0, -3),),
+        (),
+        (("r", 0, -3), ("o", 3), ("g", 1, 3), ("g", 1, 4),),
+        (),
+        (("r", 1, 4), ("g", 1, -3), ("g", 0, 4),),
+        (),
+    ),
 )
 AFTER = (
-    ("r", 1, 1, 3),
-    ("r", 0, 0, 4),
-    ("r", 0, 1, 2),
-    ("o", 4),
-    ("r", 1, 0, 2),
-    ("w", 0),
-    ("r", 1, 1, 2),
-    ("r", 0, 0, 2),
-    ("r", 0, 1, 1),
-    ("w", 1),
-    ("f", 1),
-    ("r", 0, 0, 1),
-    ("o", 5),
-    ("w", 2),
-    ("f", 0),
+    (
+        ("r", 1, -3),
+        ("r", 0, 4),
+        ("r", 0, -2),
+        ("o", 4),
+        ("r", 1, 2),
+        ("w", 0),
+        ("r", 1, -2),
+        ("r", 0, 2),
+        ("r", 0, -1),
+        ("f", 1),
+        ("r", 0, 1),
+        ("o", 5),
+        ("w", 1),
+        ("w", 2),
+        ("f", 0),
+    ),
+    (
+        ("r", 0, 4),
+        ("r", 1, 3),
+        ("r", 1, -3),
+        ("r", 0, -2),
+        ("r", 0, 3),
+        ("r", 1, 2),
+        ("o", 4),
+        ("w", 0),
+        ("r", 1, -2),
+        ("r", 0, 2),
+        ("r", 0, -1),
+        ("f", 1),
+        ("r", 0, 1),
+        ("o", 5),
+        ("w", 1),
+        ("w", 2),
+        ("f", 0),
+    ),
 )
 
 
@@ -87,15 +153,15 @@
     def dev(x=x, ylo=ylo, z=z, yh=yh, c=c):
         return (x * NYLO + ylo, z * 4 + yh * 2 + c)
 
-    def along(q, d):
-        return dev(z=(z + (a if q == 0 else -a) * d + NZ) % NZ)
+    def along(d):
+        return dev(z=(z + a * d + NZ) % NZ)
 
     sibling = dev(c=1 - c)
     partner = dev(yh=1 - yh)
     x_peer = [dev(x=(x + k) % NX) for k in range(1, NX)]
     y_peer = [dev(ylo=(ylo + k) % NYLO) for k in range(1, NYLO)]
-    steps = sorted({j - p for side in TREE for edges in side for j, p in edges.items()})
-    peers = [along(q, d) for d in steps for q in (0, 1)] + [partner, sibling, *x_peer, *y_peer]
+    steps = {abs(hop(p, e)) for core in TREE for tree in core for e, p in tree.items()}
+    peers = [along(d) for k in sorted(steps) for d in (k, -k)] + [partner, sibling, *x_peer, *y_peer]
 
     def remote(src, dst, ssem, rsem, to):
         return pltpu.make_async_remote_copy(
@@ -106,7 +172,7 @@
     y_rows = ROWS // N_REPLICA
     my_x = pl.ds(pl.multiple_of(x * x_rows, x_rows), x_rows)
     loads = [
-        pltpu.make_async_copy(tokens.at[0], tok.at[SLOT[0, 0, 0]], load_sem.at[0]),
+        pltpu.make_async_copy(tokens.at[0], tok.at[SLOT[0][OWN, 0]], load_sem.at[0]),
         pltpu.make_async_copy(gate_w, gate_v.at[0], load_sem.at[1]),
         pltpu.make_async_copy(local_up.at[0], up_v.at[0], load_sem.at[2]),
         pltpu.make_async_copy(down_w, down_v.at[0], load_sem.at[3]),
@@ -121,25 +187,22 @@
         load.start()
     pl.semaphore_wait(barrier, len(peers))
 
-    def slot(side, q, j):
-        return SLOT[side, 0 if j == 0 else q, j]
-
-    def children(side, q, p):
-        return [j for j, parent in TREE[side][q].items() if parent == p]
-
-    def gather_copy(side, q, j, src=None):
-        p, s = TREE[side][q][j], slot(side, q, j)
-        src = tok.at[slot(side, q, p)] if src is None else src
-        return remote(src, tok.at[s], ag_send.at[s], ag_recv.at[s], along(q, j - p))
-
-    def y_tokens():
-        s = SLOT[PAR, 0, 0]
+    def children(core, side, p):
+        return [e for e, parent in TREE[core][side].items() if parent == p]
+
+    def gather_copy(core, side, e, src=None):
+        p, s = TREE[core][side][e], SLOT[core][side, e]
+        src = tok.at[SLOT[core][side, p]] if src is None else src
+        return remote(src, tok.at[s], ag_send.at[s], ag_recv.at[s], along(hop(p, e)))
+
+    def y_tokens(core):
+        s = SLOT[core][PAR, 0]
         return remote(tokens.at[0], tok.at[s], y_send.at[0], ag_recv.at[s], partner)
 
-    def reduce_copy(side, q, j):
-        p, s = TREE[side][q][j], slot(side, q, j)
-        src = rs_out if children(side, q, j) else part
-        return remote(src.at[s], rs_in.at[s], rs_send.at[s], rs_recv.at[s], along(q, p - j))
+    def reduce_copy(core, side, e):
+        p, s = TREE[core][side][e], SLOT[core][side, e]
+        src = rs_out if children(core, side, e) else part
+        return remote(src.at[s], rs_in.at[s], rs_send.at[s], rs_recv.at[s], along(-hop(p, e)))
 
     def in_rows(n, size, work):
         def turn(i, carry):
@@ -148,15 +211,15 @@
 
         lax.fori_loop(0, n, turn, 0)
 
-    def sum_into(side, j, dirs, store):
-        held = [(q, child) for q in dirs for child in children(side, q, j)]
-        for q, child in held:
-            reduce_copy(side, q, child).wait_recv()
+    def sum_into(core, side, e, store):
+        held = children(core, side, e)
+        for child in held:
+            reduce_copy(core, side, child).wait_recv()
 
         def work(rows):
-            total = part[slot(side, dirs[0], j), rows, :].astype(F32)
-            for q, child in held:
-                total = total + rs_in[slot(side, q, child), rows, :].astype(F32)
+            total = part[SLOT[core][side, e], rows, :].astype(F32)
+            for child in held:
+                total = total + rs_in[SLOT[core][side, child], rows, :].astype(F32)
             store(rows, total)
 
         in_rows(4, tok.shape[1] // 4, work)
@@ -232,8 +295,8 @@
         for k, (src, dst) in enumerate(((gate_w, gate_v), (local_up.at[0], up_v), (down_w, down_v)))
     ]
 
-    def sent_all(held, sem):
-        first, second = sorted((SLOT[OWN, 0, 0], SLOT[PAR, 0, 0]))
+    def sent_all(core, held, sem):
+        first, second = sorted((SLOT[core][OWN, 0], SLOT[core][PAR, 0]))
 
         def turn(s, carry):
             remote(held.at[s], held.at[s], sem.at[s], sem.at[s], partner).wait_send()
@@ -243,12 +306,12 @@
             if low < high:
                 lax.fori_loop(low, high, turn, 0)
 
-    def wait_sends(stage):
+    def wait_sends(core, stage):
         if stage == 0:
             for weight in weights:
                 weight.wait_send()
-            y_tokens().wait_send()
-            sent_all(tok, ag_send)
+            y_tokens(core).wait_send()
+            sent_all(core, tok, ag_send)
             for k in range(3):
                 x_leg(k).wait_send()
                 y_leg(k).wait_send()
@@ -258,38 +321,33 @@
         else:
             for k in range(3):
                 x_gather(k).wait_send()
-            sent_all(part, rs_send)
+            sent_all(core, part, rs_send)
             y_final.wait_send()
 
-    def act(kind, *what):
+    def act(core, kind, *what):
         if kind == "g":
-            side, q, j = what
-            s = slot(side, q, j)
-            gather_copy(side, q, j).wait_recv()
-            for child in children(side, q, j):
-                gather_copy(side, q, child).start()
-        elif kind == "y":
-            y_tokens().wait_recv()
-            for q in (0, 1):
-                for child in children(PAR, q, 0):
-                    gather_copy(PAR, q, child).start()
+            side, e = what
+            copy = gather_copy(core, side, e) if e else y_tokens(core)
+            copy.wait_recv()
+            for child in children(core, side, e):
+                gather_copy(core, side, child).start()
         elif kind == "r":
-            side, q, j = what
-            if children(side, q, j):
+            side, e = what
+            if children(core, side, e):
 
 
                 def store(rows, total):
-                    rs_out[slot(side, q, j), rows, :] = total.astype(BF16)
-
-                sum_into(side, j, (q,), store)
-            reduce_copy(side, q, j).start()
+                    rs_out[SLOT[core][side, e], rows, :] = total.astype(BF16)
+
+                sum_into(core, side, e, store)
+            reduce_copy(core, side, e).start()
         elif kind == "f":
             if what[0] == PAR:
 
                 def store(rows, total):
                     y_out[rows, :] = total.astype(BF16)
 
-                sum_into(PAR, 0, (0, 1), store)
+                sum_into(core, PAR, 0, store)
                 y_final.start()
             else:
 
@@ -297,16 +355,20 @@
                     out_v[rows, :] = (total + y_in[rows, :].astype(F32)).astype(BF16)
 
                 y_final.wait_recv()
-                sum_into(OWN, 0, (0, 1), store)
+                sum_into(core, OWN, 0, store)
         elif kind == "o":
             outer(what[0])
         else:
-            wait_sends(what[0])
-
-    for q in (0, 1):
-        for child in children(OWN, q, 0):
-            gather_copy(OWN, q, child, tokens.at[0]).start()
-    y_tokens().start()
+            wait_sends(core, what[0])
+
+    for core in (0, 1):
+
+        @pl.when(c == core)
+        def _():
+            for child in children(core, OWN, 0):
+                gather_copy(core, OWN, child, tokens.at[0]).start()
+            y_tokens(core).start()
+
     for weight in weights:
         weight.start()
     for k in range(3):
@@ -335,9 +397,17 @@
             both = (acc[...] + total) * (0.5 * ROWS ** -0.5)
             part[pl.ds(2 * i, 2)] = both.astype(BF16).reshape(2, blk, ROWS)
 
+    def each(todo):
+        for core in (0, 1):
+            if todo[core]:
+
+                @pl.when(c == core)
+                def _():
+                    for what in todo[core]:
+                        act(core, *what)
+
     def prepare(at):
-        for what in BEFORE[at]:
-            act(*what)
+        each([BEFORE[core][at] for core in (0, 1)])
         if at == 1:
             for weight in weights:
                 weight.wait_recv()
@@ -350,13 +420,12 @@
         lax.cond(u < middle, lambda: dispatch(u, low, middle), lambda: dispatch(u, middle, high))
 
     def unit(u, carry):
-        dispatch(u, 0, len(BEFORE))
+        dispatch(u, 0, N_SLOT)
         compute(u // 2, u % 2)
         return carry
 
-    lax.fori_loop(0, len(BEFORE), unit, 0)
-    for what in AFTER:
-        act(*what)
+    lax.fori_loop(0, N_SLOT, unit, 0)
+    each(AFTER)
 
 
 def store_kernel(*refs):

time: 53.3 us -> 52.6 us (0.987)
  the two profiles are of different devices: /device:TPU:66 before, /device:TPU:2 now
where the time goes in v5:
time: 52.6 us; the launch traced here: 52.4 us
  Pallas kernels  51.8 us (98%)
  between operations  0.64 us (1%)
    pallas_call x1, Pallas kernels, body(): pl.pallas_call(kernel, out_shape=tuple((pltpu.VMEM(shape, kind) for shape...  51 us

profile of v5, /device:TPU:2, one launch (start us, length us, event | category | flops | bytes accessed | tf_op | source)
XLA Modules:
  0.0 52.4 jit_solution(13111522584866847666)
XLA Ops:
  0.6 51.0 %shard_map.102 = (bf16[128,256]{1,0:T(8,128)(2,1)S(1)}, bf16[256,896]{1,0:T(8,128)(2,1)S(1)}, f32[16,896]{1,0:T(8,128)S(1)}, f32[16,896]{1,0:T(8,128)S(1)}) custom-call(bf16[1,128,256]{2,1,0:T(8,128)(2,1)} %tokens.1, bf16[256,896]{1,0:T(8,128)(2,1)} %gate_w.1, bf16[896,256]{1,0:T(8,128)(2,1)} %down_w.1, bf16[1,256,896]{2,1,0:T(8,128)(2,1)} %local_up.1, ...), custom_call_target="tpu_custom_call" | custom-call | flops 5699999744 | bytes 3000000 | tf_op jit(solution)/shard_map/pallas_call | solution.py:455
  51.6 0.9 %shard_map.103 = (bf16[128,256]{1,0:T(8,128)(2,1)}, bf16[256,896]{1,0:T(8,128)(2,1)}, f32[16,896]{1,0:T(8,128)}, f32[16,896]{1,0:T(8,128)}) custom-call(bf16[128,256]{1,0:T(8,128)(2,1)S(1)} %get-tuple-element.12.refs_0_, bf16[256,896]{1,0:T(8,128)(2,1)S(1)} %get-tuple-element.13.refs_1_, f32[16,896]{1,0:T(8,128)S(1)} %get-tuple-element.14.refs_2_, ...), custom_call_target="tpu_custom_call" | custom-call | tf_op jit(solution)/shard_map/pallas_call | solution.py:495

commit v6 on v5

--- a/solution.py
+++ b/solution.py
@@ -61,8 +61,8 @@
 
 BEFORE = (
     (
-        (("g", 0, 1),),
-        (("g", 0, -1),),
+        (("g", 0, 1), ("g", 0, -1),),
+        (),
         (("g", 1, 0),),
         (("g", 0, 2),),
         (("g", 0, -2),),
@@ -104,11 +104,11 @@
         ("r", 0, -2),
         ("o", 4),
         ("r", 1, 2),
-        ("w", 0),
         ("r", 1, -2),
         ("r", 0, 2),
         ("r", 0, -1),
         ("f", 1),
+        ("w", 0),
         ("r", 0, 1),
         ("o", 5),
         ("w", 1),
@@ -123,11 +123,11 @@
         ("r", 0, 3),
         ("r", 1, 2),
         ("o", 4),
-        ("w", 0),
         ("r", 1, -2),
         ("r", 0, 2),
         ("r", 0, -1),
         ("f", 1),
+        ("w", 0),
         ("r", 0, 1),
         ("o", 5),
         ("w", 1),
@@ -373,8 +373,6 @@
         weight.start()
     for k in range(3):
         x_leg(k).start()
-    for load in loads[:4]:
-        load.wait()
 
     blk, width = tok.shape[1], gate_v.shape[2]
 
@@ -408,6 +406,9 @@
 
     def prepare(at):
         each([BEFORE[core][at] for core in (0, 1)])
+        if at == 0:
+            for load in loads[:4]:
+                load.wait()
         if at == 1:
             for weight in weights:
                 weight.wait_recv()

time: 52.6 us -> 52.3 us (level)
  no operation moved by 1% of the time
where the time goes in v6:
time: 52.3 us; the launch traced here: 52.2 us
  Pallas kernels  51.5 us (98%)
  between operations  0.64 us (1%)
    pallas_call x1, Pallas kernels, body(): pl.pallas_call(kernel, out_shape=tuple((pltpu.VMEM(shape, kind) for shape...  50.7 us

profile of v6, /device:TPU:2, one launch (start us, length us, event | category | flops | bytes accessed | tf_op | source)
XLA Modules:
  0.0 52.2 jit_solution(12694084630819799053)
XLA Ops:
  0.6 50.7 %shard_map.102 = (bf16[128,256]{1,0:T(8,128)(2,1)S(1)}, bf16[256,896]{1,0:T(8,128)(2,1)S(1)}, f32[16,896]{1,0:T(8,128)S(1)}, f32[16,896]{1,0:T(8,128)S(1)}) custom-call(bf16[1,128,256]{2,1,0:T(8,128)(2,1)} %tokens.1, bf16[256,896]{1,0:T(8,128)(2,1)} %gate_w.1, bf16[896,256]{1,0:T(8,128)(2,1)} %down_w.1, bf16[1,256,896]{2,1,0:T(8,128)(2,1)} %local_up.1, ...), custom_call_target="tpu_custom_call" | custom-call | flops 5699999744 | bytes 3000000 | tf_op jit(solution)/shard_map/pallas_call | solution.py:456
  51.3 0.9 %shard_map.103 = (bf16[128,256]{1,0:T(8,128)(2,1)}, bf16[256,896]{1,0:T(8,128)(2,1)}, f32[16,896]{1,0:T(8,128)}, f32[16,896]{1,0:T(8,128)}) custom-call(bf16[128,256]{1,0:T(8,128)(2,1)S(1)} %get-tuple-element.12.refs_0_, bf16[256,896]{1,0:T(8,128)(2,1)S(1)} %get-tuple-element.13.refs_1_, f32[16,896]{1,0:T(8,128)S(1)} %get-tuple-element.14.refs_2_, ...), custom_call_target="tpu_custom_call" | custom-call | tf_op jit(solution)/shard_map/pallas_call | solution.py:496

commit v7 on v6

--- a/solution.py
+++ b/solution.py
@@ -104,11 +104,11 @@
         ("r", 0, -2),
         ("o", 4),
         ("r", 1, 2),
+        ("w", 0),
         ("r", 1, -2),
         ("r", 0, 2),
         ("r", 0, -1),
         ("f", 1),
-        ("w", 0),
         ("r", 0, 1),
         ("o", 5),
         ("w", 1),
@@ -123,11 +123,11 @@
         ("r", 0, 3),
         ("r", 1, 2),
         ("o", 4),
+        ("w", 0),
         ("r", 1, -2),
+        ("f", 1),
         ("r", 0, 2),
         ("r", 0, -1),
-        ("f", 1),
-        ("w", 0),
         ("r", 0, 1),
         ("o", 5),
         ("w", 1),

time: 52.3 us -> 52.3 us (level)
  the two profiles are of different devices: /device:TPU:2 before, /device:TPU:4 now
where the time goes in v7:
time: 52.3 us; the launch traced here: 52.2 us
  Pallas kernels  51.5 us (98%)
  between operations  0.64 us (1%)
    pallas_call x1, Pallas kernels, body(): pl.pallas_call(kernel, out_shape=tuple((pltpu.VMEM(shape, kind) for shape...  50.7 us

profile of v7, /device:TPU:4, one launch (start us, length us, event | category | flops | bytes accessed | tf_op | source)
XLA Modules:
  0.0 52.2 jit_solution(11967745881516001473)
XLA Ops:
  0.6 50.7 %shard_map.102 = (bf16[128,256]{1,0:T(8,128)(2,1)S(1)}, bf16[256,896]{1,0:T(8,128)(2,1)S(1)}, f32[16,896]{1,0:T(8,128)S(1)}, f32[16,896]{1,0:T(8,128)S(1)}) custom-call(bf16[1,128,256]{2,1,0:T(8,128)(2,1)} %tokens.1, bf16[256,896]{1,0:T(8,128)(2,1)} %gate_w.1, bf16[896,256]{1,0:T(8,128)(2,1)} %down_w.1, bf16[1,256,896]{2,1,0:T(8,128)(2,1)} %local_up.1, ...), custom_call_target="tpu_custom_call" | custom-call | flops 5699999744 | bytes 3000000 | tf_op jit(solution)/shard_map/pallas_call | solution.py:456
  51.3 0.9 %shard_map.103 = (bf16[128,256]{1,0:T(8,128)(2,1)}, bf16[256,896]{1,0:T(8,128)(2,1)}, f32[16,896]{1,0:T(8,128)}, f32[16,896]{1,0:T(8,128)}) custom-call(bf16[128,256]{1,0:T(8,128)(2,1)S(1)} %get-tuple-element.12.refs_0_, bf16[256,896]{1,0:T(8,128)(2,1)S(1)} %get-tuple-element.13.refs_1_, f32[16,896]{1,0:T(8,128)S(1)} %get-tuple-element.14.refs_2_, ...), custom_call_target="tpu_custom_call" | custom-call | tf_op jit(solution)/shard_map/pallas_call | solution.py:496
